TPU v7x, 32 devices: a whole 2x2x4 slice. The times are simulated.
32 devices in a mesh: groups: 2 (over y), span: 4 (over z), batch: 4 (over x, core).
Axes of the slice: x: 2, y: 2, z: 4, core: 2. Of those that a mesh axis runs over, the one named last changes fastest.
Arguments:
- embeddings: bfloat16 [8, 512, 768], P(('groups', 'batch'), 'span'), parts along dimension 0, may hold values from -3500 to 3500
- cluster_ids: int32 [8, 512], P(('groups', 'batch'), 'span'), parts along dimension 0, may hold values from 0 to 15, as said below
Outputs:
- nearest: float32 [8, 512], P(('groups', 'batch'), 'span'), parts along dimension 0
There are 2 independent parts, one for each index of `groups`. A program takes and returns all parts, laid end to end along the dimension named above; each array names one. Nothing has to cross between parts.
Inputs may be any that keep to these rules, and one draw needn't show every extreme that they name: `cluster_ids`: on one device at most 96 rows carry ids of one residue modulo 4; in every batch some residue has exactly 96 rows on every device of the span.
All inputs are finite; a program needn't handle non-finite values.
Results may differ from a plain program's by a relative error of at most 0.00061.
Values may be sent and summed in bfloat16 or wider, within the bound.
A program may use at most 64 MiB of HBM per device.

v0:
```python
import math

import jax
import jax.numpy as jnp
from jax import lax
from jax.sharding import PartitionSpec as P


def normalize(embeddings):
    values = embeddings.astype(jnp.float32)
    inverse = lax.rsqrt(jnp.mean(values * values, axis=-1, keepdims=True) + 1e-06)
    return (values * inverse * (1.0 / math.sqrt(values.shape[-1]))).astype(jnp.bfloat16)


def pair_scores(left, right):
    return lax.dot_general(
        left, right, (((1,), (1,)), ((), ())), preferred_element_type=jnp.float32
    )


def per_device(embeddings, cluster_ids):
    normed = normalize(embeddings[0])
    member_ids = cluster_ids[0]
    row_count = normed.shape[0]
    own_index = lax.axis_index("span")
    own_rows = own_index * row_count + jnp.arange(row_count, dtype=jnp.int32)
    start_value = jnp.full((row_count,), -1.0, jnp.float32)
    piece_rows = lax.all_gather(normed, "span", axis=0, tiled=True)
    piece_ids = lax.all_gather(member_ids.astype(jnp.bfloat16), "span", axis=0, tiled=True)
    scores = pair_scores(normed, piece_rows)
    column_rows = jnp.arange(piece_rows.shape[0], dtype=jnp.int32)
    same_cluster = (member_ids[:, None] == piece_ids.astype(jnp.int32)[None, :]) & (
        own_rows[:, None] != column_rows[None, :]
    )
    nearest = jnp.maximum(start_value, jnp.max(jnp.where(same_cluster, scores, -1.0), axis=1))
    return nearest[None, :]


def solution(mesh):
    return jax.shard_map(
        per_device,
        mesh=mesh,
        in_specs=(P(("groups", "batch"), "span", None), P(("groups", "batch"), "span")),
        out_specs=P(("groups", "batch"), "span"),
        check_vma=False,
    )
```

profile of v0, /device:TPU:0, one launch (start us, length us, event | category | flops | bytes accessed | tf_op | source)
XLA Modules:
  0.0 32.3 jit_solution(1568791861424258728)
XLA Ops:
  0.0 0.0 copy-start
  0.0 1.1 %fusion.1 = f32[128]{0:T(128)S(1)} fusion(bf16[1,128,768]{2,1,0:T(8,128)(2,1)} %param.2), kind=kLoop, calls=%fused_computation.4 | loop fusion | flops 294784 | bytes 197120 | tf_op jit(solution)/shard_map/reduce_sum | solution.py:11
  1.1 0.0 copy-start.1
  1.1 0.6 %copy-done.1 = s32[1,128]{1,0:T(1,128)S(1)} copy-done((s32[1,128]{1,0:T(1,128)S(1)}, s32[1,128]{1,0:T(1,128)}, u32[]{:S(2)}) %copy-start.1) | copy-done | bytes 536
  1.8 12.5 %all-gather = bf16[4,1,128]{2,1,0:T(2,128)(2,1)S(1)} all-gather(bf16[1,1,128]{2,1,0:T(2,128)(2,1)S(1)} %convert_bitcast_fusion), channel_id=1, replica_groups=mesh['groups'=2,'span'=4,'batch'=4] {'span'}, dimensions={0}, use_global_device_ids=true | all-gather | bytes 1280 | tf_op jit(solution)/shard_map/all_gather | solution.py:29
  14.3 0.0 copy-done
  14.3 0.1 fusion.3
  14.5 16.8 %all_gather.7 = bf16[512,768]{1,0:T(8,128)(2,1)S(1)} all-gather(bf16[128,768]{1,0:T(8,128)(2,1)S(1)} %fusion.3), channel_id=1, replica_groups=mesh['groups'=2,'span'=4,'batch'=4] {'span'}, dimensions={0}, use_global_device_ids=true | all-gather | bytes 983040 | tf_op jit(solution)/shard_map/all_gather | solution.py:28
  31.3 0.5 %fusion = f32[128]{0:T(128)S(1)} fusion(bf16[128,768]{1,0:T(8,128)(2,1)S(1)} %fusion.3, bf16[512,768]{1,0:T(8,128)(2,1)S(1)} %all_gather.7, s32[128]{0:T(128)S(1)} %iota_add_fusion, s32[512]{0:T(512)S(1)} %bitcast.13, s32[128]{0:T(128)S(1)} %bitcast.14), kind=kOutput, calls=%fused_computation.1 | convolution fusion | flops 100990848 | bytes 986624 | tf_op jit(solution)/shard_map/dot_general | solution.py:16
  31.8 0.5 %maximum_bitcast_fusion = f32[1,128]{1,0:T(1,128)} fusion(f32[128]{0:T(128)S(1)} %fusion), kind=kLoop, calls=%fused_computation.9 | loop fusion | flops 128 | bytes 1024 | tf_op jit(solution)/shard_map/max;broadcast_in_dim | solution.py:35
  (4 shorter events, 0.0 us)
Async XLA Ops:
  0.0 14.3 %copy-start = (bf16[1,128,768]{2,1,0:T(8,128)(2,1)S(1)}, bf16[1,128,768]{2,1,0:T(8,128)(2,1)}, u32[]{:S(2)}) copy-start(bf16[1,128,768]{2,1,0:T(8,128)(2,1)} %param.2) | copy-start | bytes 589828
  1.1 0.7 %copy-start.1 = (s32[1,128]{1,0:T(1,128)S(1)}, s32[1,128]{1,0:T(1,128)}, u32[]{:S(2)}) copy-start(s32[1,128]{1,0:T(1,128)} %param.3) | copy-start | bytes 1540
where the time goes:
time: 32.5 us; the launch traced here: 32.3 us
  blocking collectives  29.4 us (90%)
  other arithmetic  1.77 us (5%)
  local copies, waits for them, and re-layouts  0.65 us (2%)
  matrix products  0.48 us (1%)
    all_gather x1, blocking collectives, per_device(): piece_rows = lax.all_gather(normed, 'span', axis=0, tiled=True)  16.8 us
    all_gather x1, blocking collectives, per_device(): lax.all_gather(member_ids.astype(jnp.bfloat16), 'span', axis=0, tiled=True)  12.5 us
    reduce_sum x1, other arithmetic, normalize(): jnp.mean(values * values, axis=-1, keepdims=True) + 1e-06  1.11 us

commit v1 on v0

v1 whole, which is shorter than its diff:
```python
import functools
import math

import jax
import jax.numpy as jnp
from jax import lax
from jax.experimental import pallas as pl
from jax.experimental.pallas import tpu as pltpu
from jax.sharding import PartitionSpec as P

MESH = pl.DeviceIdType.MESH
HUB_SPAN = 8


def normalize(embeddings):
    values = embeddings.astype(jnp.float32)
    inverse = lax.rsqrt(jnp.mean(values * values, axis=-1, keepdims=True) + 1e-06)
    return (values * inverse * (1.0 / math.sqrt(values.shape[-1]))).astype(jnp.bfloat16)


def pair_scores(left, right):
    return lax.dot_general(
        left, right, (((1,), (1,)), ((), ())), preferred_element_type=jnp.float32
    )


def gather_device(embeddings, cluster_ids):
    normed = normalize(embeddings[0])
    member_ids = cluster_ids[0]
    row_count = normed.shape[0]
    own_index = lax.axis_index("span")
    own_rows = own_index * row_count + jnp.arange(row_count, dtype=jnp.int32)
    piece_rows = lax.all_gather(normed, "span", axis=0, tiled=True)
    piece_ids = lax.all_gather(member_ids.astype(jnp.bfloat16), "span", axis=0, tiled=True)
    scores = pair_scores(normed, piece_rows)
    column_rows = jnp.arange(piece_rows.shape[0], dtype=jnp.int32)
    same_cluster = (member_ids[:, None] == piece_ids.astype(jnp.int32)[None, :]) & (
        own_rows[:, None] != column_rows[None, :]
    )
    nearest = jnp.max(jnp.where(same_cluster, scores, -1.0), axis=1)
    return jnp.maximum(nearest, -1.0)[None, :]


def hub_kernel(span, emb_ref, ids_ref, out_ref, raw, ids, normed, maxima,
               local_sem, send_sem, ids_send, row_sem, id_sem, back_send, back_sem):
    rows = emb_ref.shape[1]
    me = lax.axis_index("span")
    flip = lax.rem(lax.axis_index("batch"), 2)
    place = jnp.where(flip == 0, me, span - 1 - me)
    hub = span // 2

    def device(spot):
        return {"span": jnp.where(flip == 0, spot, span - 1 - spot)}

    def row_copy(spot):
        return pltpu.make_async_remote_copy(
            src_ref=emb_ref.at[0], dst_ref=raw.at[spot], send_sem=send_sem,
            recv_sem=row_sem.at[spot], device_id=device(hub), device_id_type=MESH)

    def id_copy(spot):
        return pltpu.make_async_remote_copy(
            src_ref=ids_ref, dst_ref=ids.at[spot], send_sem=ids_send,
            recv_sem=id_sem.at[spot], device_id=device(hub), device_id_type=MESH)

    def back_copy(spot):
        return pltpu.make_async_remote_copy(
            src_ref=maxima.at[spot], dst_ref=out_ref, send_sem=back_send.at[spot],
            recv_sem=back_sem, device_id=device(spot), device_id_type=MESH)

    barrier = pltpu.get_barrier_semaphore()

    @pl.when(place != hub)
    def _():
        pl.semaphore_signal(barrier, inc=1, device_id=device(hub), device_id_type=MESH)
        pl.semaphore_wait(barrier, 1)
        id_copy(place).start()
        row_copy(place).start()
        id_copy(place).wait_send()
        row_copy(place).wait_send()
        back_copy(place).wait_recv()

    @pl.when(place == hub)
    def _():
        others = [spot for spot in range(span) if spot != hub]
        for spot in others:
            pl.semaphore_signal(barrier, inc=1, device_id=device(spot), device_id_type=MESH)
        own = pltpu.make_async_copy(emb_ref.at[0], raw.at[hub], local_sem.at[0])
        own_ids = pltpu.make_async_copy(ids_ref, ids.at[hub], local_sem.at[1])
        own.start()
        own_ids.start()
        order = sorted(range(span), key=lambda spot: (abs(spot - hub), -spot))
        row_ids, column_ids, best = [], [], []
        for step, spot in enumerate(order):
            if step == 0:
                own.wait()
                own_ids.wait()
            else:
                if step == 1:
                    pl.semaphore_wait(barrier, span - 1)
                id_copy(spot).wait_recv()
                row_copy(spot).wait_recv()
            row_ids.append(ids[spot])
            column_ids.append(jnp.transpose(jnp.broadcast_to(ids[spot], (rows, rows))))
            block = normalize(raw[spot])
            normed[pl.ds(step * rows, rows), :] = block
            into = pair_scores(normed[pl.ds(0, (step + 1) * rows), :], block)
            apart = lax.broadcasted_iota(jnp.int32, (rows, rows), 0) != \
                lax.broadcasted_iota(jnp.int32, (rows, rows), 1)
            mine = jnp.where((column_ids[step] == row_ids[step]) & apart,
                             into[step * rows:, :], -1.0)
            for other in range(step):
                part = into[other * rows:(other + 1) * rows, :]
                mine = jnp.maximum(
                    mine, jnp.where(column_ids[other] == row_ids[step], part, -1.0))
            best.append(jnp.max(mine, axis=0, keepdims=True))
            if step:
                onto = pair_scores(block, normed[pl.ds(0, step * rows), :])
                for other in range(step):
                    part = onto[:, other * rows:(other + 1) * rows]
                    part = jnp.where(column_ids[step] == row_ids[other], part, -1.0)
                    best[other] = jnp.maximum(
                        best[other], jnp.max(part, axis=0, keepdims=True))
        for step, spot in reversed(list(enumerate(order))):
            if step:
                maxima[spot] = best[step]
                back_copy(spot).start()
        out_ref[...] = best[0]
        for spot in others:
            back_copy(spot).wait_send()


def hub_device(span, embeddings, cluster_ids):
    _, rows, width = embeddings.shape
    return pl.pallas_call(
        functools.partial(hub_kernel, span),
        out_shape=jax.ShapeDtypeStruct((1, rows), jnp.float32),
        in_specs=[pl.BlockSpec(memory_space=pl.ANY)] * 2,
        out_specs=pl.BlockSpec(memory_space=pltpu.VMEM),
        scratch_shapes=[
            pltpu.VMEM((span, rows, width), jnp.bfloat16),
            pltpu.VMEM((span, 1, rows), jnp.int32),
            pltpu.VMEM((span * rows, width), jnp.bfloat16),
            pltpu.VMEM((span, 1, rows), jnp.float32),
            pltpu.SemaphoreType.DMA((2,)),
            pltpu.SemaphoreType.DMA,
            pltpu.SemaphoreType.DMA,
            pltpu.SemaphoreType.DMA((span,)),
            pltpu.SemaphoreType.DMA((span,)),
            pltpu.SemaphoreType.DMA((span,)),
            pltpu.SemaphoreType.DMA,
        ],
        compiler_params=pltpu.CompilerParams(
            collective_id=0, has_side_effects=True, vmem_limit_bytes=16 * 1024 * 1024),
    )(embeddings, cluster_ids)


def solution(mesh):
    span = mesh.shape["span"]
    body = functools.partial(hub_device, span) if 1 < span <= HUB_SPAN else gather_device
    return jax.shard_map(
        body,
        mesh=mesh,
        in_specs=(P(("groups", "batch"), "span", None), P(("groups", "batch"), "span")),
        out_specs=P(("groups", "batch"), "span"),
        check_vma=False,
    )
```

time: 32.5 us -> 17 us (0.52)
  blocking collectives: 29.4 us -> 0 us
  Pallas kernels: 0 us -> 14.7 us
  other arithmetic: 1.77 us -> 0 us
  local copies, waits for them, and re-layouts: 0.65 us -> 2.09 us
  matrix products: 0.48 us -> 0 us
    all_gather x2 -> x0, blocking collectives: 29.4 us -> none  [the longest x1 16.8 us: per_device(): piece_rows = lax.all_gather(normed, 'span', axis=0, tiled=True)]
    pallas_call x0 -> x1, Pallas kernels: none -> 14.7 us  [hub_device(): pl.pallas_call(functools.partial(hub_kernel, span), out_shape=jax.ShapeDt...]
    unnamed x4 -> x5, local copies, waits for them, and re-layouts: 0.65 us -> 2.09 us
    reduce_sum x1 -> x0, other arithmetic: 1.11 us -> none  [normalize(): jnp.mean(values * values, axis=-1, keepdims=True) + 1e-06]
    another operation x1 -> x0, other arithmetic: 0.52 us -> none  [per_device(): jnp.maximum(start_value, jnp.max(jnp.where(same_cluster, scores, -1.0), a...]
    dot_general x1 -> x0, matrix products: 0.48 us -> none  [pair_scores(): lax.dot_general(left, right, (((1,), (1,)), ((), ())), preferred_element_...]
where the time goes in v1:
time: 17 us; the launch traced here: 16.8 us
  Pallas kernels  14.7 us (86%)
  local copies, waits for them, and re-layouts  2.09 us (12%)
    pallas_call x1, Pallas kernels, hub_device(): pl.pallas_call(functools.partial(hub_kernel, span), out_shape=jax.ShapeDt...  14.7 us
    unnamed x5, local copies, waits for them, and re-layouts  2.09 us

profile of v1, /device:TPU:0, one launch (start us, length us, event | category | flops | bytes accessed | tf_op | source)
XLA Modules:
  0.0 16.8 jit_solution(16884268821734064341)
XLA Ops:
  0.0 0.0 copy-start
  0.0 0.9 %copy-done = bf16[1,128,768]{2,1,0:T(8,128)(2,1)S(1)} copy-done((bf16[1,128,768]{2,1,0:T(8,128)(2,1)S(1)}, bf16[1,128,768]{2,1,0:T(8,128)(2,1)}, u32[]{:S(2)}) %copy-start) | copy-done | bytes 196632
  0.9 0.0 copy-start.1
  0.9 0.7 %copy-done.1 = s32[1,128]{1,0:T(1,128)S(1)} copy-done((s32[1,128]{1,0:T(1,128)S(1)}, s32[1,128]{1,0:T(1,128)}, u32[]{:S(2)}) %copy-start.1) | copy-done | bytes 536
  1.6 14.7 %shard_map.28 = f32[1,128]{1,0:T(1,128)S(1)} custom-call(bf16[1,128,768]{2,1,0:T(8,128)(2,1)S(1)} %copy-done, s32[1,128]{1,0:T(1,128)S(1)} %copy-done.1), custom_call_target="tpu_custom_call" | custom-call | tf_op jit(solution)/shard_map/pallas_call | solution.py:134
  16.3 0.5 %copy.4 = f32[1,128]{1,0:T(1,128)} copy(f32[1,128]{1,0:T(1,128)S(1)} %shard_map.28) | data formatting | bytes 1024
Async XLA Ops:
  0.0 0.9 %copy-start = (bf16[1,128,768]{2,1,0:T(8,128)(2,1)S(1)}, bf16[1,128,768]{2,1,0:T(8,128)(2,1)}, u32[]{:S(2)}) copy-start(bf16[1,128,768]{2,1,0:T(8,128)(2,1)} %emb_ref.1) | copy-start | bytes 589828
  0.9 0.7 %copy-start.1 = (s32[1,128]{1,0:T(1,128)S(1)}, s32[1,128]{1,0:T(1,128)}, u32[]{:S(2)}) copy-start(s32[1,128]{1,0:T(1,128)} %ids_ref.1) | copy-start | bytes 1540

commit v2 on v1

--- a/solution.py
+++ b/solution.py
@@ -45,7 +45,7 @@
                local_sem, send_sem, ids_send, row_sem, id_sem, back_send, back_sem):
     rows = emb_ref.shape[1]
     me = lax.axis_index("span")
-    flip = lax.rem(lax.axis_index("batch"), 2)
+    flip = 1 - lax.rem(lax.axis_index("batch"), 2)
     place = jnp.where(flip == 0, me, span - 1 - me)
     hub = span // 2
 
@@ -150,7 +150,7 @@
             pltpu.SemaphoreType.DMA,
         ],
         compiler_params=pltpu.CompilerParams(
-            collective_id=0, has_side_effects=True, vmem_limit_bytes=16 * 1024 * 1024),
+            collective_id=0, has_side_effects=True, vmem_limit_bytes=60 * 1024 * 1024),
     )(embeddings, cluster_ids)
 
 

time: 17 us -> 16.2 us (0.953)
  local copies, waits for them, and re-layouts: 2.09 us -> 1.19 us
  Pallas kernels: 14.7 us -> 14.9 us
    unnamed x5 -> x1, local copies, waits for them, and re-layouts: 2.09 us -> 1.19 us
where the time goes in v2:
time: 16.2 us; the launch traced here: 16.1 us
  Pallas kernels  14.9 us (92%)
  local copies, waits for them, and re-layouts  1.19 us (7%)
    pallas_call x1, Pallas kernels, hub_device(): pl.pallas_call(functools.partial(hub_kernel, span), out_shape=jax.ShapeDt...  14.9 us
    unnamed x1, local copies, waits for them, and re-layouts  1.19 us

profile of v2, /device:TPU:0, one launch (start us, length us, event | category | flops | bytes accessed | tf_op | source)
XLA Modules:
  0.0 16.1 jit_solution(879536504739281117)
XLA Ops:
  0.0 14.9 %shard_map.28 = f32[1,128]{1,0:T(1,128)} custom-call(bf16[1,128,768]{2,1,0:T(8,128)(2,1)} %emb_ref.1, s32[1,128]{1,0:T(1,128)} %ids_ref.1), custom_call_target="tpu_custom_call" | custom-call | tf_op jit(solution)/shard_map/pallas_call | solution.py:134
  14.9 1.2 %copy.4 = f32[1,128]{1,0:T(1,128)} copy(f32[1,128]{1,0:T(1,128)} %shard_map.28) | data formatting | bytes 1024

commit v3 on v2

v3 whole, which is shorter than its diff:
```python
import functools
import math

import jax
import jax.numpy as jnp
from jax import lax
from jax.experimental import pallas as pl
from jax.experimental.pallas import tpu as pltpu
from jax.sharding import PartitionSpec as P

MESH = pl.DeviceIdType.MESH
HUB_SPAN = 8
PIECES = 2


def normalize(embeddings):
    values = embeddings.astype(jnp.float32)
    inverse = lax.rsqrt(jnp.mean(values * values, axis=-1, keepdims=True) + 1e-06)
    return (values * inverse * (1.0 / math.sqrt(values.shape[-1]))).astype(jnp.bfloat16)


def pair_scores(left, right):
    return lax.dot_general(
        left, right, (((1,), (1,)), ((), ())), preferred_element_type=jnp.float32
    )


def gather_device(embeddings, cluster_ids):
    normed = normalize(embeddings[0])
    member_ids = cluster_ids[0]
    row_count = normed.shape[0]
    own_index = lax.axis_index("span")
    own_rows = own_index * row_count + jnp.arange(row_count, dtype=jnp.int32)
    piece_rows = lax.all_gather(normed, "span", axis=0, tiled=True)
    piece_ids = lax.all_gather(member_ids.astype(jnp.bfloat16), "span", axis=0, tiled=True)
    scores = pair_scores(normed, piece_rows)
    column_rows = jnp.arange(piece_rows.shape[0], dtype=jnp.int32)
    same_cluster = (member_ids[:, None] == piece_ids.astype(jnp.int32)[None, :]) & (
        own_rows[:, None] != column_rows[None, :]
    )
    nearest = jnp.max(jnp.where(same_cluster, scores, -1.0), axis=1)
    return jnp.maximum(nearest, -1.0)[None, :]


def masked_pairs(scores, column_ids, row_ids):
    return jnp.where(column_ids == row_ids, scores, -1.0)


def as_columns(row):
    return jnp.transpose(jnp.broadcast_to(row, (row.shape[1], row.shape[1])))


def within(block, column_ids, row_ids):
    rows = block.shape[0]
    apart = lax.broadcasted_iota(jnp.int32, (rows, rows), 0) != \
        lax.broadcasted_iota(jnp.int32, (rows, rows), 1)
    pairs = masked_pairs(pair_scores(block, block), column_ids, row_ids)
    return jnp.max(jnp.where(apart, pairs, -1.0), axis=0, keepdims=True)


def hub_kernel(span, pieces, emb_ref, ids_ref, out_ref, raw, ids, normed, maxima, back,
               local_sem, local_ids, send_sem, ids_send, row_sem, id_sem, back_send, back_sem):
    rows = emb_ref.shape[1]
    part = rows // pieces
    me = lax.axis_index("span")
    flip = lax.rem(lax.axis_index("batch"), 2)
    place = jnp.where(flip == 1, me, span - 1 - me)
    hub = span // 2

    def device(spot):
        return {"span": jnp.where(flip == 1, spot, span - 1 - spot)}

    def local_copy(piece):
        cut = pl.ds(piece * part, part)
        return pltpu.make_async_copy(
            emb_ref.at[0, cut], raw.at[place, cut], local_sem.at[piece])

    def local_id_copy():
        return pltpu.make_async_copy(ids_ref, ids.at[place], local_ids)

    def row_copy(spot, piece):
        cut = pl.ds(piece * part, part)
        return pltpu.make_async_remote_copy(
            src_ref=raw.at[spot, cut], dst_ref=raw.at[spot, cut], send_sem=send_sem.at[piece],
            recv_sem=row_sem.at[spot, piece], device_id=device(hub), device_id_type=MESH)

    def id_copy(spot):
        return pltpu.make_async_remote_copy(
            src_ref=ids.at[spot], dst_ref=ids.at[spot], send_sem=ids_send,
            recv_sem=id_sem.at[spot], device_id=device(hub), device_id_type=MESH)

    def back_copy(spot):
        return pltpu.make_async_remote_copy(
            src_ref=maxima.at[spot], dst_ref=back, send_sem=back_send.at[spot],
            recv_sem=back_sem, device_id=device(spot), device_id_type=MESH)

    barrier = pltpu.get_barrier_semaphore()
    local_id_copy().start()
    for piece in range(pieces):
        local_copy(piece).start()

    @pl.when(place != hub)
    def _():
        pl.semaphore_signal(barrier, inc=1, device_id=device(hub), device_id_type=MESH)
        local_id_copy().wait()
        local_copy(0).wait()
        pl.semaphore_wait(barrier, 1)
        id_copy(place).start()
        row_copy(place, 0).start()
        for piece in range(1, pieces):
            local_copy(piece).wait()
            row_copy(place, piece).start()
        own_ids = ids[place]
        own = within(normalize(raw[place]), as_columns(own_ids), own_ids)
        id_copy(place).wait_send()
        for piece in range(pieces):
            row_copy(place, piece).wait_send()
        back_copy(place).wait_recv()
        out_ref[...] = jnp.maximum(back[...], own)

    @pl.when(place == hub)
    def _():
        others = [spot for spot in range(span) if spot != hub]
        for spot in others:
            pl.semaphore_signal(barrier, inc=1, device_id=device(spot), device_id_type=MESH)
        local_id_copy().wait()
        for piece in range(pieces):
            local_copy(piece).wait()
        order = sorted(range(span), key=lambda spot: (abs(spot - hub), -spot))
        row_ids = [ids[hub]]
        block = normalize(raw[hub])
        normed[pl.ds(0, rows), :] = block
        best = [within(block, as_columns(row_ids[0]), row_ids[0])]
        pl.semaphore_wait(barrier, span - 1)
        for spot in order[1:]:
            id_copy(spot).wait_recv()
            row_ids.append(ids[spot])
        column_ids = [as_columns(row) for row in row_ids]
        for step, spot in list(enumerate(order))[1:]:
            across = []
            for piece in range(pieces):
                cut = slice(piece * part, (piece + 1) * part)
                row_copy(spot, piece).wait_recv()
                block = normalize(raw[spot, cut])
                if step < span - 1:
                    normed[pl.ds(step * rows + piece * part, part), :] = block
                scores = pair_scores(block, normed[pl.ds(0, step * rows), :])
                widest = None
                for other in range(step):
                    pairs = masked_pairs(scores[:, other * rows:(other + 1) * rows],
                                         column_ids[step][cut], row_ids[other])
                    best[other] = jnp.maximum(
                        best[other], jnp.max(pairs, axis=0, keepdims=True))
                    widest = pairs if widest is None else jnp.maximum(widest, pairs)
                across.append(widest)
            widest = jnp.transpose(jnp.concatenate(across, axis=0))
            best.append(jnp.max(widest, axis=0, keepdims=True))
        for step, spot in reversed(list(enumerate(order))):
            if step:
                maxima[spot] = best[step]
                back_copy(spot).start()
        out_ref[...] = best[0]
        for spot in others:
            back_copy(spot).wait_send()


def hub_device(span, embeddings, cluster_ids):
    _, rows, width = embeddings.shape
    pieces = PIECES if rows % (16 * PIECES) == 0 else 1
    return pl.pallas_call(
        functools.partial(hub_kernel, span, pieces),
        out_shape=pltpu.VMEM((1, rows), jnp.float32),
        in_specs=[pl.BlockSpec(memory_space=pl.ANY)] * 2,
        out_specs=pl.BlockSpec(memory_space=pltpu.VMEM),
        scratch_shapes=[
            pltpu.VMEM((span, rows, width), jnp.bfloat16),
            pltpu.VMEM((span, 1, rows), jnp.int32),
            pltpu.VMEM(((span - 1) * rows, width), jnp.bfloat16),
            pltpu.VMEM((span, 1, rows), jnp.float32),
            pltpu.VMEM((1, rows), jnp.float32),
            pltpu.SemaphoreType.DMA((pieces,)),
            pltpu.SemaphoreType.DMA,
            pltpu.SemaphoreType.DMA((pieces,)),
            pltpu.SemaphoreType.DMA,
            pltpu.SemaphoreType.DMA((span, pieces)),
            pltpu.SemaphoreType.DMA((span,)),
            pltpu.SemaphoreType.DMA((span,)),
            pltpu.SemaphoreType.DMA,
        ],
        compiler_params=pltpu.CompilerParams(
            collective_id=0, has_side_effects=True, vmem_limit_bytes=60 * 1024 * 1024),
    )(embeddings, cluster_ids)


def solution(mesh):
    span = mesh.shape["span"]
    body = functools.partial(hub_device, span) if 1 < span <= HUB_SPAN else gather_device
    return jax.shard_map(
        body,
        mesh=mesh,
        in_specs=(P(("groups", "batch"), "span", None), P(("groups", "batch"), "span")),
        out_specs=P(("groups", "batch"), "span"),
        check_vma=False,
    )
```

time: 16.2 us -> 15.1 us (0.932)
  local copies, waits for them, and re-layouts: 1.19 us -> 0.51 us
  Pallas kernels: 14.9 us -> 14.5 us
    unnamed x1, local copies, waits for them, and re-layouts: 1.19 us -> 0.51 us
    pallas_call x1, Pallas kernels: 14.9 us -> 14.5 us  [hub_device(): pl.pallas_call(functools.partial(hub_kernel, span, pieces), out_shape=plt...]
where the time goes in v3:
time: 15.1 us; the launch traced here: 15 us
  Pallas kernels  14.5 us (96%)
  local copies, waits for them, and re-layouts  0.51 us (3%)
    pallas_call x1, Pallas kernels, hub_device(): pl.pallas_call(functools.partial(hub_kernel, span, pieces), out_shape=plt...  14.5 us
    unnamed x1, local copies, waits for them, and re-layouts  0.51 us

profile of v3, /device:TPU:0, one launch (start us, length us, event | category | flops | bytes accessed | tf_op | source)
XLA Modules:
  0.0 15.0 jit_solution(6575330499456951659)
XLA Ops:
  0.0 14.5 %shard_map.28 = f32[1,128]{1,0:T(1,128)S(1)} custom-call(bf16[1,128,768]{2,1,0:T(8,128)(2,1)} %emb_ref.1, s32[1,128]{1,0:T(1,128)} %ids_ref.1), custom_call_target="tpu_custom_call" | custom-call | tf_op jit(solution)/shard_map/pallas_call | solution.py:170
  14.5 0.5 %copy.4 = f32[1,128]{1,0:T(1,128)} copy(f32[1,128]{1,0:T(1,128)S(1)} %shard_map.28) | data formatting | bytes 1024

commit v4 on v3

--- a/solution.py
+++ b/solution.py
@@ -10,7 +10,7 @@
 
 MESH = pl.DeviceIdType.MESH
 HUB_SPAN = 8
-PIECES = 2
+PIECES = 1
 
 
 def normalize(embeddings):

time: 15.1 us -> 14.4 us (0.954)
  Pallas kernels: 14.5 us -> 13.7 us
    pallas_call x1, Pallas kernels: 14.5 us -> 13.7 us  [hub_device(): pl.pallas_call(functools.partial(hub_kernel, span, pieces), out_shape=plt...]
where the time goes in v4:
time: 14.4 us; the launch traced here: 14.2 us
  Pallas kernels  13.7 us (95%)
  local copies, waits for them, and re-layouts  0.51 us (4%)
    pallas_call x1, Pallas kernels, hub_device(): pl.pallas_call(functools.partial(hub_kernel, span, pieces), out_shape=plt...  13.7 us
    unnamed x1, local copies, waits for them, and re-layouts  0.51 us

profile of v4, /device:TPU:0, one launch (start us, length us, event | category | flops | bytes accessed | tf_op | source)
XLA Modules:
  0.0 14.2 jit_solution(13133707310256288409)
XLA Ops:
  0.0 13.7 %shard_map.28 = f32[1,128]{1,0:T(1,128)S(1)} custom-call(bf16[1,128,768]{2,1,0:T(8,128)(2,1)} %emb_ref.1, s32[1,128]{1,0:T(1,128)} %ids_ref.1), custom_call_target="tpu_custom_call" | custom-call | tf_op jit(solution)/shard_map/pallas_call | solution.py:170
  13.7 0.5 %copy.4 = f32[1,128]{1,0:T(1,128)} copy(f32[1,128]{1,0:T(1,128)S(1)} %shard_map.28) | data formatting | bytes 1024

commit v5 on v4

--- a/solution.py
+++ b/solution.py
@@ -10,7 +10,6 @@
 
 MESH = pl.DeviceIdType.MESH
 HUB_SPAN = 8
-PIECES = 1
 
 
 def normalize(embeddings):
@@ -58,31 +57,35 @@
     return jnp.max(jnp.where(apart, pairs, -1.0), axis=0, keepdims=True)
 
 
-def hub_kernel(span, pieces, emb_ref, ids_ref, out_ref, raw, ids, normed, maxima, back,
+def hub_kernel(span, emb_ref, ids_ref, out_ref, raw, ids, normed, maxima, back,
                local_sem, local_ids, send_sem, ids_send, row_sem, id_sem, back_send, back_sem):
     rows = emb_ref.shape[1]
-    part = rows // pieces
     me = lax.axis_index("span")
     flip = lax.rem(lax.axis_index("batch"), 2)
     place = jnp.where(flip == 1, me, span - 1 - me)
     hub = span // 2
 
+    def slot(spot):
+        away = spot - hub
+        if isinstance(spot, int):
+            order = min(2 * away - 1 if away > 0 else -2 * away, span - 1)
+            return pl.ds(order * rows, rows)
+        order = jnp.minimum(jnp.where(away > 0, 2 * away - 1, -2 * away), span - 1)
+        return pl.ds(pl.multiple_of(order * rows, rows), rows)
+
     def device(spot):
         return {"span": jnp.where(flip == 1, spot, span - 1 - spot)}
 
-    def local_copy(piece):
-        cut = pl.ds(piece * part, part)
-        return pltpu.make_async_copy(
-            emb_ref.at[0, cut], raw.at[place, cut], local_sem.at[piece])
+    def local_copy():
+        return pltpu.make_async_copy(emb_ref.at[0], raw, local_sem)
 
     def local_id_copy():
         return pltpu.make_async_copy(ids_ref, ids.at[place], local_ids)
 
-    def row_copy(spot, piece):
-        cut = pl.ds(piece * part, part)
+    def row_copy(spot):
         return pltpu.make_async_remote_copy(
-            src_ref=raw.at[spot, cut], dst_ref=raw.at[spot, cut], send_sem=send_sem.at[piece],
-            recv_sem=row_sem.at[spot, piece], device_id=device(hub), device_id_type=MESH)
+            src_ref=normed.at[slot(spot)], dst_ref=normed.at[slot(spot)], send_sem=send_sem,
+            recv_sem=row_sem.at[spot], device_id=device(hub), device_id_type=MESH)
 
     def id_copy(spot):
         return pltpu.make_async_remote_copy(
@@ -96,25 +99,22 @@
 
     barrier = pltpu.get_barrier_semaphore()
     local_id_copy().start()
-    for piece in range(pieces):
-        local_copy(piece).start()
+    local_copy().start()
 
     @pl.when(place != hub)
     def _():
         pl.semaphore_signal(barrier, inc=1, device_id=device(hub), device_id_type=MESH)
         local_id_copy().wait()
-        local_copy(0).wait()
+        local_copy().wait()
+        block = normalize(raw[...])
+        normed[slot(place), :] = block
         pl.semaphore_wait(barrier, 1)
         id_copy(place).start()
-        row_copy(place, 0).start()
-        for piece in range(1, pieces):
-            local_copy(piece).wait()
-            row_copy(place, piece).start()
+        row_copy(place).start()
         own_ids = ids[place]
-        own = within(normalize(raw[place]), as_columns(own_ids), own_ids)
+        own = within(block, as_columns(own_ids), own_ids)
         id_copy(place).wait_send()
-        for piece in range(pieces):
-            row_copy(place, piece).wait_send()
+        row_copy(place).wait_send()
         back_copy(place).wait_recv()
         out_ref[...] = jnp.maximum(back[...], own)
 
@@ -124,12 +124,11 @@
         for spot in others:
             pl.semaphore_signal(barrier, inc=1, device_id=device(spot), device_id_type=MESH)
         local_id_copy().wait()
-        for piece in range(pieces):
-            local_copy(piece).wait()
+        local_copy().wait()
         order = sorted(range(span), key=lambda spot: (abs(spot - hub), -spot))
         row_ids = [ids[hub]]
-        block = normalize(raw[hub])
-        normed[pl.ds(0, rows), :] = block
+        block = normalize(raw[...])
+        normed[slot(hub), :] = block
         best = [within(block, as_columns(row_ids[0]), row_ids[0])]
         pl.semaphore_wait(barrier, span - 1)
         for spot in order[1:]:
@@ -137,24 +136,16 @@
             row_ids.append(ids[spot])
         column_ids = [as_columns(row) for row in row_ids]
         for step, spot in list(enumerate(order))[1:]:
-            across = []
-            for piece in range(pieces):
-                cut = slice(piece * part, (piece + 1) * part)
-                row_copy(spot, piece).wait_recv()
-                block = normalize(raw[spot, cut])
-                if step < span - 1:
-                    normed[pl.ds(step * rows + piece * part, part), :] = block
-                scores = pair_scores(block, normed[pl.ds(0, step * rows), :])
-                widest = None
-                for other in range(step):
-                    pairs = masked_pairs(scores[:, other * rows:(other + 1) * rows],
-                                         column_ids[step][cut], row_ids[other])
-                    best[other] = jnp.maximum(
-                        best[other], jnp.max(pairs, axis=0, keepdims=True))
-                    widest = pairs if widest is None else jnp.maximum(widest, pairs)
-                across.append(widest)
-            widest = jnp.transpose(jnp.concatenate(across, axis=0))
-            best.append(jnp.max(widest, axis=0, keepdims=True))
+            row_copy(spot).wait_recv()
+            scores = pair_scores(normed[slot(spot), :], normed[pl.ds(0, step * rows), :])
+            widest = None
+            for other in range(step):
+                pairs = masked_pairs(scores[:, other * rows:(other + 1) * rows],
+                                     column_ids[step], row_ids[other])
+                best[other] = jnp.maximum(
+                    best[other], jnp.max(pairs, axis=0, keepdims=True))
+                widest = pairs if widest is None else jnp.maximum(widest, pairs)
+            best.append(jnp.max(jnp.transpose(widest), axis=0, keepdims=True))
         for step, spot in reversed(list(enumerate(order))):
             if step:
                 maxima[spot] = best[step]
@@ -166,23 +157,22 @@
 
 def hub_device(span, embeddings, cluster_ids):
     _, rows, width = embeddings.shape
-    pieces = PIECES if rows % (16 * PIECES) == 0 else 1
     return pl.pallas_call(
-        functools.partial(hub_kernel, span, pieces),
+        functools.partial(hub_kernel, span),
         out_shape=pltpu.VMEM((1, rows), jnp.float32),
         in_specs=[pl.BlockSpec(memory_space=pl.ANY)] * 2,
         out_specs=pl.BlockSpec(memory_space=pltpu.VMEM),
         scratch_shapes=[
-            pltpu.VMEM((span, rows, width), jnp.bfloat16),
+            pltpu.VMEM((rows, width), jnp.bfloat16),
             pltpu.VMEM((span, 1, rows), jnp.int32),
-            pltpu.VMEM(((span - 1) * rows, width), jnp.bfloat16),
+            pltpu.VMEM((span * rows, width), jnp.bfloat16),
             pltpu.VMEM((span, 1, rows), jnp.float32),
             pltpu.VMEM((1, rows), jnp.float32),
-            pltpu.SemaphoreType.DMA((pieces,)),
             pltpu.SemaphoreType.DMA,
-            pltpu.SemaphoreType.DMA((pieces,)),
             pltpu.SemaphoreType.DMA,
-            pltpu.SemaphoreType.DMA((span, pieces)),
+            pltpu.SemaphoreType.DMA,
+            pltpu.SemaphoreType.DMA,
+            pltpu.SemaphoreType.DMA((span,)),
             pltpu.SemaphoreType.DMA((span,)),
             pltpu.SemaphoreType.DMA((span,)),
             pltpu.SemaphoreType.DMA,

time: 14.4 us -> 14.4 us (level)
  no operation moved by 1% of the time
where the time goes in v5:
time: 14.4 us; the launch traced here: 14.2 us
  Pallas kernels  13.7 us (95%)
  local copies, waits for them, and re-layouts  0.51 us (4%)
    pallas_call x1, Pallas kernels, hub_device(): pl.pallas_call(functools.partial(hub_kernel, span), out_shape=pltpu.VMEM(...  13.7 us
    unnamed x1, local copies, waits for them, and re-layouts  0.51 us

profile of v5, /device:TPU:0, one launch (start us, length us, event | category | flops | bytes accessed | tf_op | source)
XLA Modules:
  0.0 14.2 jit_solution(1091698812913927747)
XLA Ops:
  0.0 13.7 %shard_map.28 = f32[1,128]{1,0:T(1,128)S(1)} custom-call(bf16[1,128,768]{2,1,0:T(8,128)(2,1)} %emb_ref.1, s32[1,128]{1,0:T(1,128)} %ids_ref.1), custom_call_target="tpu_custom_call" | custom-call | tf_op jit(solution)/shard_map/pallas_call | solution.py:160
  13.7 0.5 %copy.4 = f32[1,128]{1,0:T(1,128)} copy(f32[1,128]{1,0:T(1,128)S(1)} %shard_map.28) | data formatting | bytes 1024

commit v6 on v5

--- a/solution.py
+++ b/solution.py
@@ -137,19 +137,26 @@
         column_ids = [as_columns(row) for row in row_ids]
         for step, spot in list(enumerate(order))[1:]:
             row_copy(spot).wait_recv()
-            scores = pair_scores(normed[slot(spot), :], normed[pl.ds(0, step * rows), :])
+            block = normed[slot(spot), :]
+            last = step == span - 1
+            if not last:
+                scores = pair_scores(block, normed[pl.ds(0, step * rows), :])
             widest = None
-            for other in range(step):
-                pairs = masked_pairs(scores[:, other * rows:(other + 1) * rows],
-                                     column_ids[step], row_ids[other])
+            for other in (*range(1, step), 0):
+                if last:
+                    part = pair_scores(block, normed[slot(order[other]), :])
+                else:
+                    part = scores[:, other * rows:(other + 1) * rows]
+                pairs = masked_pairs(part, column_ids[step], row_ids[other])
                 best[other] = jnp.maximum(
                     best[other], jnp.max(pairs, axis=0, keepdims=True))
                 widest = pairs if widest is None else jnp.maximum(widest, pairs)
+                if last and other:
+                    maxima[order[other]] = best[other]
+                    back_copy(order[other]).start()
             best.append(jnp.max(jnp.transpose(widest), axis=0, keepdims=True))
-        for step, spot in reversed(list(enumerate(order))):
-            if step:
-                maxima[spot] = best[step]
-                back_copy(spot).start()
+        maxima[order[-1]] = best[-1]
+        back_copy(order[-1]).start()
         out_ref[...] = best[0]
         for spot in others:
             back_copy(spot).wait_send()

time: 14.4 us -> 14.2 us (0.986)
  Pallas kernels: 13.7 us -> 13.5 us
    pallas_call x1, Pallas kernels: 13.7 us -> 13.5 us  [hub_device(): pl.pallas_call(functools.partial(hub_kernel, span), out_shape=pltpu.VMEM(...]
where the time goes in v6:
time: 14.2 us; the launch traced here: 14 us
  Pallas kernels  13.5 us (95%)
  local copies, waits for them, and re-layouts  0.51 us (4%)
    pallas_call x1, Pallas kernels, hub_device(): pl.pallas_call(functools.partial(hub_kernel, span), out_shape=pltpu.VMEM(...  13.5 us
    unnamed x1, local copies, waits for them, and re-layouts  0.51 us

profile of v6, /device:TPU:0, one launch (start us, length us, event | category | flops | bytes accessed | tf_op | source)
XLA Modules:
  0.0 14.0 jit_solution(7613842247211726231)
XLA Ops:
  0.0 13.5 %shard_map.28 = f32[1,128]{1,0:T(1,128)S(1)} custom-call(bf16[1,128,768]{2,1,0:T(8,128)(2,1)} %emb_ref.1, s32[1,128]{1,0:T(1,128)} %ids_ref.1), custom_call_target="tpu_custom_call" | custom-call | tf_op jit(solution)/shard_map/pallas_call | solution.py:167
  13.5 0.5 %copy.4 = f32[1,128]{1,0:T(1,128)} copy(f32[1,128]{1,0:T(1,128)S(1)} %shard_map.28) | data formatting | bytes 1024

commit v7 on v6

--- a/solution.py
+++ b/solution.py
@@ -60,18 +60,24 @@
 def hub_kernel(span, emb_ref, ids_ref, out_ref, raw, ids, normed, maxima, back,
                local_sem, local_ids, send_sem, ids_send, row_sem, id_sem, back_send, back_sem):
     rows = emb_ref.shape[1]
+    half = rows // 2
     me = lax.axis_index("span")
     flip = lax.rem(lax.axis_index("batch"), 2)
     place = jnp.where(flip == 1, me, span - 1 - me)
     hub = span // 2
 
-    def slot(spot):
+    def slot(spot, piece=None):
         away = spot - hub
         if isinstance(spot, int):
             order = min(2 * away - 1 if away > 0 else -2 * away, span - 1)
-            return pl.ds(order * rows, rows)
+            start = order * rows
+            if piece is None:
+                return pl.ds(start, rows)
+            return pl.ds(start + piece * half, half)
         order = jnp.minimum(jnp.where(away > 0, 2 * away - 1, -2 * away), span - 1)
-        return pl.ds(pl.multiple_of(order * rows, rows), rows)
+        if piece is None:
+            return pl.ds(pl.multiple_of(order * rows, rows), rows)
+        return pl.ds(pl.multiple_of(order * rows + piece * half, half), half)
 
     def device(spot):
         return {"span": jnp.where(flip == 1, spot, span - 1 - spot)}
@@ -82,10 +88,11 @@
     def local_id_copy():
         return pltpu.make_async_copy(ids_ref, ids.at[place], local_ids)
 
-    def row_copy(spot):
+    def row_copy(spot, piece):
         return pltpu.make_async_remote_copy(
-            src_ref=normed.at[slot(spot)], dst_ref=normed.at[slot(spot)], send_sem=send_sem,
-            recv_sem=row_sem.at[spot], device_id=device(hub), device_id_type=MESH)
+            src_ref=normed.at[slot(spot, piece)], dst_ref=normed.at[slot(spot, piece)],
+            send_sem=send_sem.at[piece],
+            recv_sem=row_sem.at[spot, piece], device_id=device(hub), device_id_type=MESH)
 
     def id_copy(spot):
         return pltpu.make_async_remote_copy(
@@ -106,15 +113,17 @@
         pl.semaphore_signal(barrier, inc=1, device_id=device(hub), device_id_type=MESH)
         local_id_copy().wait()
         local_copy().wait()
-        block = normalize(raw[...])
-        normed[slot(place), :] = block
         pl.semaphore_wait(barrier, 1)
         id_copy(place).start()
-        row_copy(place).start()
+        for piece in range(2):
+            normed[slot(place, piece), :] = normalize(raw[pl.ds(piece * half, half), :])
+            row_copy(place, piece).start()
+        block = normed[slot(place), :]
         own_ids = ids[place]
         own = within(block, as_columns(own_ids), own_ids)
         id_copy(place).wait_send()
-        row_copy(place).wait_send()
+        for piece in range(2):
+            row_copy(place, piece).wait_send()
         back_copy(place).wait_recv()
         out_ref[...] = jnp.maximum(back[...], own)
 
@@ -136,7 +145,8 @@
             row_ids.append(ids[spot])
         column_ids = [as_columns(row) for row in row_ids]
         for step, spot in list(enumerate(order))[1:]:
-            row_copy(spot).wait_recv()
+            for piece in range(2):
+                row_copy(spot, piece).wait_recv()
             block = normed[slot(spot), :]
             last = step == span - 1
             if not last:
@@ -177,9 +187,9 @@
             pltpu.VMEM((1, rows), jnp.float32),
             pltpu.SemaphoreType.DMA,
             pltpu.SemaphoreType.DMA,
-            pltpu.SemaphoreType.DMA,
-            pltpu.SemaphoreType.DMA,
-            pltpu.SemaphoreType.DMA((span,)),
+            pltpu.SemaphoreType.DMA((2,)),
+            pltpu.SemaphoreType.DMA,
+            pltpu.SemaphoreType.DMA((span, 2)),
             pltpu.SemaphoreType.DMA((span,)),
             pltpu.SemaphoreType.DMA((span,)),
             pltpu.SemaphoreType.DMA,

time: 14.2 us -> 14.2 us (level)
  no operation moved by 1% of the time
where the time goes in v7:
time: 14.2 us; the launch traced here: 14.1 us
  Pallas kernels  13.5 us (95%)
  local copies, waits for them, and re-layouts  0.51 us (4%)
    pallas_call x1, Pallas kernels, hub_device(): pl.pallas_call(functools.partial(hub_kernel, span), out_shape=pltpu.VMEM(...  13.5 us
    unnamed x1, local copies, waits for them, and re-layouts  0.51 us

profile of v7, /device:TPU:0, one launch (start us, length us, event | category | flops | bytes accessed | tf_op | source)
XLA Modules:
  0.0 14.1 jit_solution(16042907709625263553)
XLA Ops:
  0.0 13.5 %shard_map.28 = f32[1,128]{1,0:T(1,128)S(1)} custom-call(bf16[1,128,768]{2,1,0:T(8,128)(2,1)} %emb_ref.1, s32[1,128]{1,0:T(1,128)} %ids_ref.1), custom_call_target="tpu_custom_call" | custom-call | tf_op jit(solution)/shard_map/pallas_call | solution.py:177
  13.5 0.5 %copy.4 = f32[1,128]{1,0:T(1,128)} copy(f32[1,128]{1,0:T(1,128)S(1)} %shard_map.28) | data formatting | bytes 1024
